TPU v7x, 512 devices: a whole 4x4x16 slice. The times are simulated.
512 devices in a mesh: row: 16 (over x, y), col: 32 (over z, core).
Axes of the slice: x: 4, y: 4, z: 16, core: 2. Of those that a mesh axis runs over, the one named last changes fastest.
Arguments:
- species: float32 [512, 256, 2048], P(None, 'col', 'row'), may hold values from -26 to 26, as said below
- start_basis: float32 [512, 256], replicated, may hold values from -6 to 6
Outputs:
- core_fibers: float32 [256, 256, 2048], P('row', 'col')
- basis: float32 [512, 256], replicated
Inputs may be any that keep to these rules, and one draw needn't show every extreme that they name: `species`: entries of the slab.
All inputs are finite; a program needn't handle non-finite values.
Results may differ from a plain program's by a relative error of at most 0.00019.
Values sent between devices are 32-bit elements; how exact they have to be, the bound alone decides.
No kernel may reach another device: no remote copies, remote signals or barrier semaphores. Data moves between devices by JAX's collectives and lax.ppermute only.
A program may use at most 64 MiB of HBM per device.

v0:
```python
import jax
import jax.numpy as jnp
from jax import lax
from jax.sharding import PartitionSpec as P

ITERS = 2


def orthonormalize(applied):
    inner_gram = jnp.dot(
        applied.T, applied, precision=lax.Precision.HIGHEST, preferred_element_type=jnp.float32
    )
    small_lower = jnp.linalg.cholesky(inner_gram)
    return jax.scipy.linalg.solve_triangular(small_lower, applied.T, lower=True).T


def power_steps(tri_lower, start_basis):
    current = start_basis
    for sweep_number in range(ITERS):
        halfway = jnp.dot(
            tri_lower.T,
            current,
            precision=lax.Precision.HIGHEST,
            preferred_element_type=jnp.float32,
        )
        applied = jnp.dot(
            tri_lower, halfway, precision=lax.Precision.HIGHEST, preferred_element_type=jnp.float32
        )
        current = orthonormalize(applied)
    return current


def shards(species, start_basis):
    width_x, cells_z, cells_y = species.shape
    fibers = species.reshape(width_x, cells_z * cells_y)
    local_gram = jnp.dot(
        fibers, fibers.T, precision=lax.Precision.HIGHEST, preferred_element_type=jnp.float32
    )
    gram_sum = lax.psum(local_gram, ("row", "col"))
    basis = power_steps(jnp.linalg.cholesky(gram_sum), start_basis)
    core_flat = jnp.dot(
        basis.T, fibers, precision=lax.Precision.HIGHEST, preferred_element_type=jnp.float32
    )
    core_block = core_flat.reshape(basis.shape[1], cells_z, cells_y)
    core_fibers = lax.all_to_all(core_block, "row", split_axis=0, concat_axis=2, tiled=True)
    return (core_fibers, basis)


def solution(mesh):
    in_specs = (P(None, "col", "row"), P())
    out_specs = (P("row", "col", None), P())
    return jax.shard_map(shards, mesh=mesh, in_specs=in_specs, out_specs=out_specs, check_vma=False)
```

profile of v0, /device:TPU:1, one launch (start us, length us, event | category | flops | bytes accessed | tf_op | source)
XLA Modules:
  0.0 744.2 jit_solution(14799633142379794219)
XLA Ops:
  7.2 7.1 fusion.2
  14.4 2.1 copy.41
  16.4 2.3 copy.25
  18.8 468.0 %all-reduce.4.cloned.1.call-done = f32[512,512]{0,1:T(8,128)} async-done(((f32[512,512]{0,1:T(8,128)}), f32[512,512]{0,1:T(8,128)}) %all-reduce.4.cloned.1.call-update) | async-done | bytes 1048592 | tf_op jit(solution)/shard_map/psum | solution.py:39
  489.7 11.7 %cholesky.136 = f32[128,128]{1,0:T(8,128)S(1)} custom-call(f32[128,128]{1,0:T(8,128)S(1)} %cholesky.407), custom_call_target="Cholesky" | custom-call | tf_op jit(solution)/shard_map/jit(cholesky)/cholesky | solution.py:40
  501.4 9.8 %custom-call.32 = f32[1,128,128]{1,2,0:T(8,128)S(1)} custom-call(f32[1,128,128]{2,1,0:T(8,128)S(1)} %get-tuple-element.62), custom_call_target="InvertDiagBlocksLowerTriangular" | custom-call | tf_op jit(solution)/shard_map/jit(cholesky)/cholesky | solution.py:40
  513.9 11.7 %cholesky.159 = f32[128,128]{1,0:T(8,128)S(1)} custom-call(f32[128,128]{1,0:T(8,128)S(1)} %cholesky.411), custom_call_target="Cholesky" | custom-call | tf_op jit(solution)/shard_map/jit(cholesky)/cholesky | solution.py:40
  525.6 10.0 %custom-call.33 = f32[1,128,128]{1,2,0:T(8,128)S(1)} custom-call(f32[1,128,128]{2,1,0:T(8,128)S(1)} %get-tuple-element.59), custom_call_target="InvertDiagBlocksLowerTriangular" | custom-call | tf_op jit(solution)/shard_map/jit(cholesky)/cholesky | solution.py:40
  537.1 11.7 %cholesky.294 = f32[128,128]{1,0:T(8,128)S(1)} custom-call(f32[128,128]{1,0:T(8,128)S(1)} %cholesky.416), custom_call_target="Cholesky" | custom-call | tf_op jit(solution)/shard_map/jit(cholesky)/cholesky | solution.py:40
  549.5 9.8 %custom-call.39 = f32[1,128,128]{1,2,0:T(8,128)S(1)} custom-call(f32[1,128,128]{2,1,0:T(8,128)S(1)} %get-tuple-element.56), custom_call_target="InvertDiagBlocksLowerTriangular" | custom-call | tf_op jit(solution)/shard_map/jit(cholesky)/cholesky/custom-call.9 | solution.py:40
  560.8 11.7 %cholesky.307 = f32[128,128]{1,0:T(8,128)S(1)} custom-call(f32[128,128]{1,0:T(8,128)S(1)} %convolution_subtract_fusion.6), custom_call_target="Cholesky" | custom-call | tf_op jit(solution)/shard_map/jit(cholesky)/cholesky | solution.py:40
  580.2 11.7 %cholesky.357 = f32[128,128]{1,0:T(8,128)S(1)} custom-call(f32[128,128]{1,0:T(8,128)S(1)} %cholesky.420), custom_call_target="Cholesky" | custom-call | tf_op jit(solution)/shard_map/jit(cholesky)/cholesky | solution.py:13
  592.6 9.8 %custom-call.40 = f32[1,128,128]{1,2,0:T(8,128)S(1)} custom-call(f32[1,128,128]{2,1,0:T(8,128)S(1)} %get-tuple-element.52), custom_call_target="InvertDiagBlocksLowerTriangular" | custom-call | tf_op jit(solution)/shard_map/jit(cholesky)/cholesky/custom-call.9 | solution.py:13
  603.0 11.8 %cholesky.367 = f32[128,128]{1,0:T(8,128)S(1)} custom-call(f32[128,128]{1,0:T(8,128)S(1)} %convolution_subtract_fusion.5), custom_call_target="Cholesky" | custom-call | tf_op jit(solution)/shard_map/jit(cholesky)/cholesky | solution.py:13
  616.9 4.0 while.4
  620.9 19.7 %custom-call.41 = f32[2,128,128]{1,2,0:T(8,128)S(1)} custom-call(f32[2,128,128]{2,1,0:T(8,128)S(1)} %get-tuple-element.19), custom_call_target="InvertDiagBlocksLowerTriangular" | custom-call | tf_op jit(solution)/shard_map/jit(_solve_triangular)/triangular_solve | solution.py:14
  645.5 11.7 %cholesky.384 = f32[128,128]{1,0:T(8,128)S(1)} custom-call(f32[128,128]{1,0:T(8,128)S(1)} %cholesky.423), custom_call_target="Cholesky" | custom-call | tf_op jit(solution)/shard_map/jit(cholesky)/cholesky | solution.py:13
  657.9 9.8 %custom-call.42 = f32[1,128,128]{1,2,0:T(8,128)S(1)} custom-call(f32[1,128,128]{2,1,0:T(8,128)S(1)} %get-tuple-element.48), custom_call_target="InvertDiagBlocksLowerTriangular" | custom-call | tf_op jit(solution)/shard_map/jit(cholesky)/cholesky/custom-call.9 | solution.py:13
  668.2 11.9 %cholesky.394 = f32[128,128]{1,0:T(8,128)S(1)} custom-call(f32[128,128]{1,0:T(8,128)S(1)} %convolution_subtract_fusion.4), custom_call_target="Cholesky" | custom-call | tf_op jit(solution)/shard_map/jit(cholesky)/cholesky | solution.py:13
  682.1 4.0 while.5
  686.1 19.7 %custom-call.43 = f32[2,128,128]{1,2,0:T(8,128)S(1)} custom-call(f32[2,128,128]{2,1,0:T(8,128)S(1)} %get-tuple-element.20), custom_call_target="InvertDiagBlocksLowerTriangular" | custom-call | tf_op jit(solution)/shard_map/jit(_solve_triangular)/triangular_solve | solution.py:14
  707.3 3.5 fusion.11
  712.4 6.2 all-to-all-start
  719.6 16.4 %all-to-all-done = f32[256,8,128]{2,1,0:T(8,128)S(1)} async-done(((f32[256,8,128]{2,1,0:T(8,128)}), f32[256,8,128]{2,1,0:T(8,128)S(1)}, u32[]{:S(2)}, u32[]{:S(2)}) %all-to-all-start) | async-done | bytes 1048608 | tf_op jit(solution)/shard_map/all_to_all | solution.py:45
  (81 shorter events, 36.1 us)
Async XLA Ops:
  7.2 569.2 %copy-start = (f32[512,256]{1,0:T(8,128)S(1)}, f32[512,256]{1,0:T(8,128)}, u32[]{:S(2)}) copy-start(f32[512,256]{1,0:T(8,128)} %param.8) | copy-start | bytes 1572868
  7.2 479.6 %all-reduce.4.cloned.1.call-start = ((), (), s32[]{:S(2)}) async-start(), calls=%async_computation.1 | async-start | bytes 2097152 | tf_op jit(solution)/shard_map/psum | solution.py:39
  486.8 1.7 copy-start.1
  488.7 1.0 copy-start.2
  712.4 23.7 %all-to-all-start = ((f32[256,8,128]{2,1,0:T(8,128)}), f32[256,8,128]{2,1,0:T(8,128)S(1)}, u32[]{:S(2)}, u32[]{:S(2)}) async-start(f32[256,8,128]{2,1,0:T(8,128)} %copy.26), calls=%async_computation | async-start | bytes 2097152 | tf_op jit(solution)/shard_map/all_to_all | solution.py:45
Sparse Core Ops, SparseCore 0:
  14.5 472.2 all-reduce.3
where the time goes:
time: 749 us; the launch traced here: 744 us
  waiting for transfers between devices  484 us (65%)
  other arithmetic  188 us (25%)
  matrix products  26.7 us (4%)
  between operations  19.8 us (3%)
  local copies, waits for them, and re-layouts  19.1 us (3%)
    psum x1, waiting for transfers between devices, shards(): gram_sum = lax.psum(local_gram, ('row', 'col'))  468 us
    another operation x14, other arithmetic, shards(): basis = power_steps(jnp.linalg.cholesky(gram_sum), start_basis)  78.5 us
    another operation x14, other arithmetic, orthonormalize(): small_lower = jnp.linalg.cholesky(inner_gram)  69.5 us
    another operation x5, other arithmetic, orthonormalize(): jax.scipy.linalg.solve_triangular(small_lower, applied.T, lower=True)  39.4 us
    all_to_all x1, waiting for transfers between devices, shards(): lax.all_to_all(core_block, 'row', split_axis=0, concat_axis=2, tiled=True)  16.4 us
  transfers between devices with their start and end apart: 2, of which 2 were waited for; matrix products, arithmetic and copies ran while one was open for 1% of the time, Pallas kernels for 0%

commit v1 on v0

--- a/solution.py
+++ b/solution.py
@@ -42,7 +42,10 @@
         basis.T, fibers, precision=lax.Precision.HIGHEST, preferred_element_type=jnp.float32
     )
     core_block = core_flat.reshape(basis.shape[1], cells_z, cells_y)
-    core_fibers = lax.all_to_all(core_block, "row", split_axis=0, concat_axis=2, tiled=True)
+    core_fibers = jnp.concatenate(
+        lax.all_to_all(jnp.stack(jnp.split(core_block, lax.axis_size("row"), axis=0)), "row", 0, 0),
+        axis=2,
+    )
     return (core_fibers, basis)
 
 

time: 749 us -> 763 us (1.019)
    unnamed x8 -> x39, local copies, waits for them, and re-layouts: 4.03 us -> 11.8 us
  transfers between devices with their start and end apart: 2 -> 2, of which waited for: 2 -> 2; matrix products, arithmetic and copies ran while one was open for 1% -> 0% of each run, Pallas kernels for 0% -> 0%
where the time goes in v1:
time: 763 us; the launch traced here: 754 us
  waiting for transfers between devices  489 us (64%)
  other arithmetic  189 us (25%)
  matrix products  26.5 us (3%)
  local copies, waits for them, and re-layouts  23.6 us (3%)
  between operations  19.9 us (3%)
    psum x1, waiting for transfers between devices, shards(): gram_sum = lax.psum(local_gram, ('row', 'col'))  472 us
    another operation x14, other arithmetic, shards(): basis = power_steps(jnp.linalg.cholesky(gram_sum), start_basis)  79 us
    another operation x14, other arithmetic, orthonormalize(): small_lower = jnp.linalg.cholesky(inner_gram)  69.5 us
    another operation x5, other arithmetic, orthonormalize(): jax.scipy.linalg.solve_triangular(small_lower, applied.T, lower=True)  39.8 us
    all_to_all x1, waiting for transfers between devices, shards(): lax.all_to_all(jnp.stack(jnp.split(core_block, lax.axis_size('row'), axis...  16.5 us
  transfers between devices with their start and end apart: 2, of which 2 were waited for; matrix products, arithmetic and copies ran while one was open for 0% of the time, Pallas kernels for 0%

profile of v1, /device:TPU:1, one launch (start us, length us, event | category | flops | bytes accessed | tf_op | source)
XLA Modules:
  0.0 753.8 jit_solution(17678819968121579425)
XLA Ops:
  7.2 7.1 fusion.5
  14.4 472.2 %all-reduce.4.cloned.1.call-done = f32[512,512]{0,1:T(8,128)} async-done(((f32[512,512]{0,1:T(8,128)}), f32[512,512]{0,1:T(8,128)}) %all-reduce.4.cloned.1.call-update) | async-done | bytes 1048592 | tf_op jit(solution)/shard_map/psum | solution.py:39
  486.5 1.6 copy.7
  489.4 11.7 %cholesky.136 = f32[128,128]{1,0:T(8,128)S(1)} custom-call(f32[128,128]{1,0:T(8,128)S(1)} %cholesky.407), custom_call_target="Cholesky" | custom-call | tf_op jit(solution)/shard_map/jit(cholesky)/cholesky | solution.py:40
  501.2 9.8 %custom-call.32 = f32[1,128,128]{1,2,0:T(8,128)S(1)} custom-call(f32[1,128,128]{2,1,0:T(8,128)S(1)} %get-tuple-element.76), custom_call_target="InvertDiagBlocksLowerTriangular" | custom-call | tf_op jit(solution)/shard_map/jit(cholesky)/cholesky | solution.py:40
  513.6 12.2 %cholesky.159 = f32[128,128]{1,0:T(8,128)S(1)} custom-call(f32[128,128]{1,0:T(8,128)S(1)} %cholesky.411), custom_call_target="Cholesky" | custom-call | tf_op jit(solution)/shard_map/jit(cholesky)/cholesky | solution.py:40
  525.8 9.8 %custom-call.33 = f32[1,128,128]{1,2,0:T(8,128)S(1)} custom-call(f32[1,128,128]{2,1,0:T(8,128)S(1)} %get-tuple-element.73), custom_call_target="InvertDiagBlocksLowerTriangular" | custom-call | tf_op jit(solution)/shard_map/jit(cholesky)/cholesky | solution.py:40
  537.2 11.7 %cholesky.294 = f32[128,128]{1,0:T(8,128)S(1)} custom-call(f32[128,128]{1,0:T(8,128)S(1)} %cholesky.416), custom_call_target="Cholesky" | custom-call | tf_op jit(solution)/shard_map/jit(cholesky)/cholesky | solution.py:40
  549.7 9.8 %custom-call.39 = f32[1,128,128]{1,2,0:T(8,128)S(1)} custom-call(f32[1,128,128]{2,1,0:T(8,128)S(1)} %get-tuple-element.70), custom_call_target="InvertDiagBlocksLowerTriangular" | custom-call | tf_op jit(solution)/shard_map/jit(cholesky)/cholesky/custom-call.9 | solution.py:40
  560.9 11.9 %cholesky.307 = f32[128,128]{1,0:T(8,128)S(1)} custom-call(f32[128,128]{1,0:T(8,128)S(1)} %convolution_subtract_fusion.6), custom_call_target="Cholesky" | custom-call | tf_op jit(solution)/shard_map/jit(cholesky)/cholesky | solution.py:40
  580.1 11.7 %cholesky.357 = f32[128,128]{1,0:T(8,128)S(1)} custom-call(f32[128,128]{1,0:T(8,128)S(1)} %cholesky.420), custom_call_target="Cholesky" | custom-call | tf_op jit(solution)/shard_map/jit(cholesky)/cholesky | solution.py:13
  591.9 10.0 %custom-call.40 = f32[1,128,128]{1,2,0:T(8,128)S(1)} custom-call(f32[1,128,128]{2,1,0:T(8,128)S(1)} %get-tuple-element.66), custom_call_target="InvertDiagBlocksLowerTriangular" | custom-call | tf_op jit(solution)/shard_map/jit(cholesky)/cholesky/custom-call.9 | solution.py:13
  602.4 11.7 %cholesky.367 = f32[128,128]{1,0:T(8,128)S(1)} custom-call(f32[128,128]{1,0:T(8,128)S(1)} %convolution_subtract_fusion.5), custom_call_target="Cholesky" | custom-call | tf_op jit(solution)/shard_map/jit(cholesky)/cholesky | solution.py:13
  616.8 4.0 while.4
  617.4 1.4 bitcast_dynamic-update-slice_fusion.20
  620.8 20.1 %custom-call.41 = f32[2,128,128]{1,2,0:T(8,128)S(1)} custom-call(f32[2,128,128]{2,1,0:T(8,128)S(1)} %get-tuple-element.19), custom_call_target="InvertDiagBlocksLowerTriangular" | custom-call | tf_op jit(solution)/shard_map/jit(_solve_triangular)/triangular_solve | solution.py:14
  645.8 11.7 %cholesky.384 = f32[128,128]{1,0:T(8,128)S(1)} custom-call(f32[128,128]{1,0:T(8,128)S(1)} %cholesky.423), custom_call_target="Cholesky" | custom-call | tf_op jit(solution)/shard_map/jit(cholesky)/cholesky | solution.py:13
  657.6 9.8 %custom-call.42 = f32[1,128,128]{1,2,0:T(8,128)S(1)} custom-call(f32[1,128,128]{2,1,0:T(8,128)S(1)} %get-tuple-element.62), custom_call_target="InvertDiagBlocksLowerTriangular" | custom-call | tf_op jit(solution)/shard_map/jit(cholesky)/cholesky/custom-call.9 | solution.py:13
  667.9 11.9 %cholesky.394 = f32[128,128]{1,0:T(8,128)S(1)} custom-call(f32[128,128]{1,0:T(8,128)S(1)} %convolution_subtract_fusion.4), custom_call_target="Cholesky" | custom-call | tf_op jit(solution)/shard_map/jit(cholesky)/cholesky | solution.py:13
  682.4 4.0 while.5
  686.4 19.7 %custom-call.43 = f32[2,128,128]{1,2,0:T(8,128)S(1)} custom-call(f32[2,128,128]{2,1,0:T(8,128)S(1)} %get-tuple-element.20), custom_call_target="InvertDiagBlocksLowerTriangular" | custom-call | tf_op jit(solution)/shard_map/jit(_solve_triangular)/triangular_solve | solution.py:14
  707.6 3.7 fusion
  721.9 6.2 all-to-all-start
  729.2 16.5 %all-to-all-done = f32[16,16,8,128]{3,2,1,0:T(8,128)S(1)} async-done(((f32[16,16,8,128]{3,2,1,0:T(8,128)}), f32[16,16,8,128]{3,2,1,0:T(8,128)S(1)}, u32[]{:S(2)}, u32[]{:S(2)}) %all-to-all-start) | async-done | bytes 1048608 | tf_op jit(solution)/shard_map/all_to_all | solution.py:46
  (111 shorter events, 41.6 us)
Async XLA Ops:
  7.2 569.5 %copy-start = (f32[512,256]{1,0:T(8,128)S(1)}, f32[512,256]{1,0:T(8,128)}, u32[]{:S(2)}) copy-start(f32[512,256]{1,0:T(8,128)} %param.8) | copy-start | bytes 1572868
  7.2 479.4 %all-reduce.4.cloned.1.call-start = ((), (), s32[]{:S(2)}) async-start(), calls=%async_computation.1 | async-start | bytes 2097152 | tf_op jit(solution)/shard_map/psum | solution.py:39
  486.5 1.7 copy-start.1
  488.4 1.0 copy-start.2
  721.9 23.7 %all-to-all-start = ((f32[16,16,8,128]{3,2,1,0:T(8,128)}), f32[16,16,8,128]{3,2,1,0:T(8,128)S(1)}, u32[]{:S(2)}, u32[]{:S(2)}) async-start(f32[16,16,8,128]{3,2,1,0:T(8,128)} %bitcast_dynamic-update-slice_fusion.2), calls=%async_computation | async-start | bytes 2097152 | tf_op jit(solution)/shard_map/all_to_all | solution.py:46
Sparse Core Ops, SparseCore 0:
  14.5 472.0 all-reduce.3

commit v2 on v0

--- a/solution.py
+++ b/solution.py
@@ -36,7 +36,7 @@
     local_gram = jnp.dot(
         fibers, fibers.T, precision=lax.Precision.HIGHEST, preferred_element_type=jnp.float32
     )
-    gram_sum = lax.psum(local_gram, ("row", "col"))
+    gram_sum = lax.psum(lax.psum(local_gram, "row"), "col")
     basis = power_steps(jnp.linalg.cholesky(gram_sum), start_basis)
     core_flat = jnp.dot(
         basis.T, fibers, precision=lax.Precision.HIGHEST, preferred_element_type=jnp.float32

time: 749 us -> 610 us (0.81)
  waiting for transfers between devices: 484 us -> 345 us
    psum x1 -> x2, waiting for transfers between devices: 468 us -> 331 us  [shards(): gram_sum = lax.psum(lax.psum(local_gram, 'row'), 'col')]
  transfers between devices with their start and end apart: 2 -> 3, of which waited for: 2 -> 3; matrix products, arithmetic and copies ran while one was open for 1% -> 1% of each run, Pallas kernels for 0% -> 0%
where the time goes in v2:
time: 610 us; the launch traced here: 605 us
  waiting for transfers between devices  345 us (57%)
  other arithmetic  188 us (31%)
  matrix products  26.7 us (4%)
  between operations  19.8 us (3%)
  local copies, waits for them, and re-layouts  19.1 us (3%)
  starting transfers between devices  6.61 us (1%)
    psum x2, waiting for transfers between devices, shards(): gram_sum = lax.psum(lax.psum(local_gram, 'row'), 'col')  331 us
    another operation x14, other arithmetic, shards(): basis = power_steps(jnp.linalg.cholesky(gram_sum), start_basis)  78.5 us
    another operation x14, other arithmetic, orthonormalize(): small_lower = jnp.linalg.cholesky(inner_gram)  69.5 us
    another operation x5, other arithmetic, orthonormalize(): jax.scipy.linalg.solve_triangular(small_lower, applied.T, lower=True)  39.4 us
    all_to_all x1, waiting for transfers between devices, shards(): lax.all_to_all(core_block, 'row', split_axis=0, concat_axis=2, tiled=True)  14 us
  transfers between devices with their start and end apart: 3, of which 3 were waited for; matrix products, arithmetic and copies ran while one was open for 1% of the time, Pallas kernels for 0%

profile of v2, /device:TPU:1, one launch (start us, length us, event | category | flops | bytes accessed | tf_op | source)
XLA Modules:
  0.0 604.8 jit_solution(14311546948960078555)
XLA Ops:
  7.2 7.1 %fusion.2 = f32[512,512]{0,1:T(8,128)} fusion(f32[512,8,128]{2,1,0:T(8,128)} %param.7), kind=kOutput, calls=%fused_computation.7 | convolution fusion | flops 3221225472 | bytes 3145728 | tf_op jit(solution)/shard_map/dot_general | solution.py:36
  14.4 121.7 %all-reduce.5.cloned.1.call-done = f32[512,512]{0,1:T(8,128)} async-done(((f32[512,512]{0,1:T(8,128)}), f32[512,512]{0,1:T(8,128)}) %all-reduce.5.cloned.1.call-update) | async-done | bytes 1048592 | tf_op jit(solution)/shard_map/psum | solution.py:39
  138.2 2.3 copy.25
  140.5 208.9 %all-reduce.7.cloned.1.call-done = f32[512,512]{0,1:T(8,128)} async-done(((f32[512,512]{0,1:T(8,128)}), f32[512,512]{0,1:T(8,128)}) %all-reduce.7.cloned.1.call-update) | async-done | bytes 1048592 | tf_op jit(solution)/shard_map/psum | solution.py:39
  352.4 11.7 %cholesky.136 = f32[128,128]{1,0:T(8,128)S(1)} custom-call(f32[128,128]{1,0:T(8,128)S(1)} %cholesky.407), custom_call_target="Cholesky" | custom-call | tf_op jit(solution)/shard_map/jit(cholesky)/cholesky | solution.py:40
  364.1 9.8 %custom-call.32 = f32[1,128,128]{1,2,0:T(8,128)S(1)} custom-call(f32[1,128,128]{2,1,0:T(8,128)S(1)} %get-tuple-element.62), custom_call_target="InvertDiagBlocksLowerTriangular" | custom-call | tf_op jit(solution)/shard_map/jit(cholesky)/cholesky | solution.py:40
  376.6 11.7 %cholesky.159 = f32[128,128]{1,0:T(8,128)S(1)} custom-call(f32[128,128]{1,0:T(8,128)S(1)} %cholesky.411), custom_call_target="Cholesky" | custom-call | tf_op jit(solution)/shard_map/jit(cholesky)/cholesky | solution.py:40
  388.3 10.0 %custom-call.33 = f32[1,128,128]{1,2,0:T(8,128)S(1)} custom-call(f32[1,128,128]{2,1,0:T(8,128)S(1)} %get-tuple-element.59), custom_call_target="InvertDiagBlocksLowerTriangular" | custom-call | tf_op jit(solution)/shard_map/jit(cholesky)/cholesky | solution.py:40
  399.9 11.7 %cholesky.294 = f32[128,128]{1,0:T(8,128)S(1)} custom-call(f32[128,128]{1,0:T(8,128)S(1)} %cholesky.416), custom_call_target="Cholesky" | custom-call | tf_op jit(solution)/shard_map/jit(cholesky)/cholesky | solution.py:40
  412.3 9.8 %custom-call.39 = f32[1,128,128]{1,2,0:T(8,128)S(1)} custom-call(f32[1,128,128]{2,1,0:T(8,128)S(1)} %get-tuple-element.56), custom_call_target="InvertDiagBlocksLowerTriangular" | custom-call | tf_op jit(solution)/shard_map/jit(cholesky)/cholesky/custom-call.9 | solution.py:40
  423.5 11.7 %cholesky.307 = f32[128,128]{1,0:T(8,128)S(1)} custom-call(f32[128,128]{1,0:T(8,128)S(1)} %convolution_subtract_fusion.6), custom_call_target="Cholesky" | custom-call | tf_op jit(solution)/shard_map/jit(cholesky)/cholesky | solution.py:40
  442.9 11.7 %cholesky.357 = f32[128,128]{1,0:T(8,128)S(1)} custom-call(f32[128,128]{1,0:T(8,128)S(1)} %cholesky.420), custom_call_target="Cholesky" | custom-call | tf_op jit(solution)/shard_map/jit(cholesky)/cholesky | solution.py:13
  455.3 9.8 %custom-call.40 = f32[1,128,128]{1,2,0:T(8,128)S(1)} custom-call(f32[1,128,128]{2,1,0:T(8,128)S(1)} %get-tuple-element.52), custom_call_target="InvertDiagBlocksLowerTriangular" | custom-call | tf_op jit(solution)/shard_map/jit(cholesky)/cholesky/custom-call.9 | solution.py:13
  465.7 11.8 %cholesky.367 = f32[128,128]{1,0:T(8,128)S(1)} custom-call(f32[128,128]{1,0:T(8,128)S(1)} %convolution_subtract_fusion.5), custom_call_target="Cholesky" | custom-call | tf_op jit(solution)/shard_map/jit(cholesky)/cholesky | solution.py:13
  479.6 4.0 while.4
  483.6 19.7 %custom-call.41 = f32[2,128,128]{1,2,0:T(8,128)S(1)} custom-call(f32[2,128,128]{2,1,0:T(8,128)S(1)} %get-tuple-element.19), custom_call_target="InvertDiagBlocksLowerTriangular" | custom-call | tf_op jit(solution)/shard_map/jit(_solve_triangular)/triangular_solve | solution.py:14
  508.2 11.7 %cholesky.384 = f32[128,128]{1,0:T(8,128)S(1)} custom-call(f32[128,128]{1,0:T(8,128)S(1)} %cholesky.423), custom_call_target="Cholesky" | custom-call | tf_op jit(solution)/shard_map/jit(cholesky)/cholesky | solution.py:13
  520.6 9.8 %custom-call.42 = f32[1,128,128]{1,2,0:T(8,128)S(1)} custom-call(f32[1,128,128]{2,1,0:T(8,128)S(1)} %get-tuple-element.48), custom_call_target="InvertDiagBlocksLowerTriangular" | custom-call | tf_op jit(solution)/shard_map/jit(cholesky)/cholesky/custom-call.9 | solution.py:13
  530.9 11.9 %cholesky.394 = f32[128,128]{1,0:T(8,128)S(1)} custom-call(f32[128,128]{1,0:T(8,128)S(1)} %convolution_subtract_fusion.4), custom_call_target="Cholesky" | custom-call | tf_op jit(solution)/shard_map/jit(cholesky)/cholesky | solution.py:13
  544.8 4.0 while.5
  548.8 19.7 %custom-call.43 = f32[2,128,128]{1,2,0:T(8,128)S(1)} custom-call(f32[2,128,128]{2,1,0:T(8,128)S(1)} %get-tuple-element.20), custom_call_target="InvertDiagBlocksLowerTriangular" | custom-call | tf_op jit(solution)/shard_map/jit(_solve_triangular)/triangular_solve | solution.py:14
  570.0 3.5 fusion.11
  575.1 6.5 %all-to-all-start = ((f32[256,8,128]{2,1,0:T(8,128)}), f32[256,8,128]{2,1,0:T(8,128)S(1)}, u32[]{:S(2)}, u32[]{:S(2)}) async-start(f32[256,8,128]{2,1,0:T(8,128)} %copy.26), calls=%async_computation | async-start | bytes 2097152 | tf_op jit(solution)/shard_map/all_to_all | solution.py:45
  582.7 14.0 %all-to-all-done = f32[256,8,128]{2,1,0:T(8,128)S(1)} async-done(((f32[256,8,128]{2,1,0:T(8,128)}), f32[256,8,128]{2,1,0:T(8,128)S(1)}, u32[]{:S(2)}, u32[]{:S(2)}) %all-to-all-start) | async-done | bytes 1048608 | tf_op jit(solution)/shard_map/all_to_all | solution.py:45
  (84 shorter events, 38.2 us)
Async XLA Ops:
  7.2 431.9 %copy-start = (f32[512,256]{1,0:T(8,128)S(1)}, f32[512,256]{1,0:T(8,128)}, u32[]{:S(2)}) copy-start(f32[512,256]{1,0:T(8,128)} %param.8) | copy-start | bytes 1572868
  7.2 128.9 %all-reduce.5.cloned.1.call-start = ((), (), s32[]{:S(2)}) async-start(), calls=%async_computation.1 | async-start | bytes 2097152 | tf_op jit(solution)/shard_map/psum | solution.py:39
  14.4 335.1 %all-reduce.7.cloned.1.call-start = ((), (), s32[]{:S(2)}) async-start(), calls=%async_computation.2 | async-start | bytes 2097152 | tf_op jit(solution)/shard_map/psum | solution.py:39
  349.5 1.7 copy-start.1
  351.4 1.0 copy-start.2
  575.1 21.5 %all-to-all-start = ((f32[256,8,128]{2,1,0:T(8,128)}), f32[256,8,128]{2,1,0:T(8,128)S(1)}, u32[]{:S(2)}, u32[]{:S(2)}) async-start(f32[256,8,128]{2,1,0:T(8,128)} %copy.26), calls=%async_computation | async-start | bytes 2097152 | tf_op jit(solution)/shard_map/all_to_all | solution.py:45
Sparse Core Ops, SparseCore 0:
  14.5 121.5 all-reduce.4
  138.4 210.9 all-reduce.6
